TPU v7x, 32 devices: a whole 2x2x4 slice. The times are simulated.
32 devices in a mesh: tm: 8 (over z, core), row: 4 (over y, x).
Axes of the slice: x: 2, y: 2, z: 4, core: 2. Of those that a mesh axis runs over, the one named last changes fastest.
Arguments:
- covariance: float32 [8, 1024, 1024], P('tm', 'row'), as said below
- precision: float32 [8, 1024, 1024], P('tm', 'row'), as said below
- band_weight: float32 [8, 5, 1024], P('tm'), may hold values from -0.5 to 0.5
- band_offset: int32 [8, 5], P('tm'), may hold values from -64 to 64, as said below
- prior_mean: float32 [8, 1024], P('tm', 'row'), may hold values from -6 to 6
- innovation: float32 [8, 128], P('tm'), may hold values from -6 to 6
- seen_sites: int32 [8, 128], P('tm'), may hold values from 0 to 511, as said below
Outputs:
- smoother_gain: float32 [8, 1024, 1024], P('tm', 'row')
- smoother_shift: float32 [8, 1024], P('tm', 'row')
- smoother_spread: float32 [8, 1024, 1024], P('tm', 'row')
Inputs may be any that keep to these rules, and one draw needn't show every extreme that they name: `covariance`: each block's matrix is symmetric. `precision`: each block's matrix is symmetric. `band_offset`: the offsets of one block are distinct, and one of them has magnitude 64. `seen_sites`: the sites of one step are distinct.
All inputs are finite; a program needn't handle non-finite values.
Results may differ from a plain program's by a relative error of at most 0.0003.
Values sent between devices are 32-bit elements; how exact they have to be, the bound alone decides.
A program may use at most 64 MiB of HBM per device.

v0:
```python
import functools

import jax
import jax.numpy as jnp
from jax import lax
from jax.experimental import pallas as pl
from jax.experimental.pallas import tpu as pltpu
from jax.sharding import PartitionSpec as P

NBAND = 5
REACH = 64
SPAN = 3
TILE = 256
EDGE = 128
VEC = 16

MESH = pl.DeviceIdType.MESH
F32 = jnp.float32
BF16 = jnp.bfloat16


def split(value):
    high = value.astype(BF16)
    return high, (value - high.astype(F32)).astype(BF16)


def dot3(left, right):
    (lh, ll), (rh, rl) = left, right
    one = functools.partial(jnp.dot, preferred_element_type=F32)
    return one(lh, rh) + (one(lh, rl) + one(ll, rh))


def dot3t(left, right):
    (lh, ll), (rh, rl) = left, right

    def one(a, b):
        return lax.dot_general(a, b, (((1,), (1,)), ((), ())), preferred_element_type=F32)

    return one(lh, rh) + (one(lh, rl) + one(ll, rh))


def kernel(
    n, n_row,
    offsets, cov_rows, inv_rows, weights, prior, innovation, seen,
    gain_out, shift_out, spread_out,
    cov_land, inv_land, cov_h, cov_l, inv_h, inv_l, ft_h, ft_l,
    x_in, x_keep, w_keep, v_in, v_out, a_h, a_l, pad_h, pad_l, acc, pad_acc,
    prior_all, f_h, f_l, h_h, h_l, part, vec_in, vec_out,
    g_send, g_recv, p_send, p_recv, x_send, x_recv, home_send, home_recv,
    v_send, v_recv, vec_send, vec_recv,
):
    tm = lax.axis_index("tm")
    row = lax.axis_index("row")
    rows, columns = cov_rows.shape
    tiles = columns // TILE

    def at(index, size):
        return pl.ds(pl.multiple_of(index * size, size), size)

    barrier = pltpu.get_barrier_semaphore()

    def greet(t, r):
        pl.semaphore_signal(barrier, inc=1, device_id=(t, r), device_id_type=MESH)

    for d in range(1, n_row):
        greet(tm, lax.rem(row + d, n_row))
    for d in range(1, SPAN + 1):
        pl.when(tm + d < n)(lambda d=d: greet(tm + d, row))
        pl.when(tm - d >= 0)(lambda d=d: greet(tm - d, row))
    pl.semaphore_wait(
        barrier, n_row - 1 + jnp.minimum(tm, SPAN) + jnp.minimum(n - 1 - tm, SPAN)
    )

    square = n_row == 4
    if square:
        x, y = lax.rem(row, 2), row // 2
        r1, r2, r3 = 2 * y + 1 - x, 2 * (1 - y) + x, 2 * (1 - y) + 1 - x
    half = rows // 2

    def pieces(m, src, land):
        def copy(c, to, rsl, csl, drow):
            return pltpu.make_async_remote_copy(
                src_ref=src.at[rsl, csl], dst_ref=land.at[drow, csl],
                send_sem=g_send.at[m, c], recv_sem=g_recv.at[m, c],
                device_id=(tm, to), device_id_type=MESH,
            )

        every = pl.ds(0, rows)
        if not square:
            return [
                copy(d - 1, lax.rem(row + d, n_row), every, pl.ds(0, columns), at(row, rows))
                for d in range(1, n_row)
            ]
        right = pl.ds(pl.multiple_of(r3 * rows + half, half), half)
        upper = pl.ds(pl.multiple_of(row * rows, rows), half)
        mine = at(row, rows)
        return [
            copy(0, r1, every, at(row, rows), mine),
            copy(1, r2, every, at(row, rows), mine),
            copy(2, r3, every, at(row, rows), mine),
            copy(3, r1, every, at(r2, rows), mine),
            copy(4, r2, every, at(r1, rows), mine),
            copy(5, r1, pl.ds(0, half), at(r3, rows), upper),
            copy(6, r2, every, right, mine),
        ]

    def fill(src, land, high, low):
        def put(rsl, csl, value):
            h, l = split(value)
            high[rsl, csl] = h
            low[rsl, csl] = l

        if not square:
            land[at(row, rows), :] = src[...]

            def every(r, carry):
                rsl = at(r, TILE)
                put(rsl, pl.ds(0, columns), land[rsl, :])
                return carry

            lax.fori_loop(0, columns // TILE, every, 0)
            return
        put(at(row, rows), pl.ds(0, columns), src[...])
        for r in (r1, r2, r3):
            put(at(r, rows), at(row, rows), src[:, at(r, rows)].T)
            put(at(r, rows), at(r, rows), land[at(r, rows), at(r, rows)])
        for r in (r1, r2):
            block = land[at(r, rows), at(r3, rows)]
            put(at(r, rows), at(r3, rows), block)
            put(at(r3, rows), at(r, rows), block.T)
        upper = pl.ds(pl.multiple_of(r1 * rows, rows), half)
        lower = pl.ds(pl.multiple_of(r1 * rows + half, half), half)
        block = land[upper, at(r2, rows)]
        put(upper, at(r2, rows), block)
        put(at(r2, rows), upper, block.T)
        block = land[at(r2, rows), lower]
        put(at(r2, rows), lower, block)
        put(lower, at(r2, rows), block.T)

    inv_copies = pieces(0, inv_rows, inv_land)
    cov_copies = pieces(1, cov_rows, cov_land)
    for c in inv_copies:
        c.start()

    prior_all[row] = prior[...]
    prior_copies = [
        pltpu.make_async_remote_copy(
            src_ref=prior, dst_ref=prior_all.at[row],
            send_sem=p_send.at[d - 1], recv_sem=p_recv.at[d - 1],
            device_id=(tm, lax.rem(row + d, n_row)), device_id_type=MESH,
        )
        for d in range(1, n_row)
    ]
    for c in prior_copies:
        c.start()

    window = TILE + 2 * EDGE
    apart = lax.broadcasted_iota(jnp.int32, (window, TILE), 0) - (
        lax.broadcasted_iota(jnp.int32, (window, TILE), 1) + EDGE
    )
    for t in range(tiles):
        total = jnp.zeros((window, TILE), F32)
        for b in range(NBAND):
            scale = weights[b : b + 1, t * TILE : (t + 1) * TILE]
            total = total + jnp.where(apart == offsets[0, b], scale, 0.0)
        h, l = split(total)
        ft_h[t] = h
        ft_l[t] = l

    zeros = jnp.zeros((rows, EDGE), BF16)
    for ref in (pad_h, pad_l):
        ref[:, :EDGE] = zeros
        ref[:, EDGE + columns :] = zeros

    def full(t):
        return pl.ds(pl.multiple_of(t * TILE, TILE), TILE)

    def x_copy(s, t):
        return pltpu.make_async_remote_copy(
            src_ref=x_keep.at[s, :, full(t)], dst_ref=x_in.at[s, :, full(t)],
            send_sem=x_send.at[s, t], recv_sem=x_recv.at[s, t],
            device_id=(tm + 1, row), device_id_type=MESH,
        )

    def home_copy(s, t):
        return pltpu.make_async_remote_copy(
            src_ref=x_keep.at[s, :, full(t)], dst_ref=gain_out.at[:, full(t)],
            send_sem=home_send.at[s, t], recv_sem=home_recv.at[t],
            device_id=(tm - s, row), device_id_type=MESH,
        )

    def v_copy(s, t):
        return pltpu.make_async_remote_copy(
            src_ref=v_out.at[s, :, full(t)], dst_ref=v_in.at[s, :, full(t)],
            send_sem=v_send.at[s, t], recv_sem=v_recv.at[s, t],
            device_id=(tm - 1, row), device_id_type=MESH,
        )

    def vec_copy(s):
        return pltpu.make_async_remote_copy(
            src_ref=vec_out.at[s], dst_ref=vec_in.at[s],
            send_sem=vec_send.at[s], recv_sem=vec_recv.at[s],
            device_id=(tm - 1, row), device_id_type=MESH,
        )

    def goes_up(s):
        return (tm >= s) & (s < SPAN) & (tm + 1 < n)

    def goes_home(s):
        return (tm >= s) & (s > 0) & ((s == SPAN) | (tm == n - 1))

    def goes_down(s):
        return (tm >= s) & (s > 0)

    def band_step(s):
        h, l = split(w_keep[s])
        pad_h[:, EDGE : EDGE + columns] = h
        pad_l[:, EDGE : EDGE + columns] = l
        for t in range(tiles):
            wide = slice(t * TILE, t * TILE + window)
            h, l = split(dot3((pad_h[:, wide], pad_l[:, wide]), (ft_h[t], ft_l[t])))
            a_h[:, t * TILE : (t + 1) * TILE] = h
            a_l[:, t * TILE : (t + 1) * TILE] = l

    def gain_step(s):
        def one(t, carry):
            x_keep[s, :, full(t)] = dot3(
                (a_h[...], a_l[...]), (inv_h[:, full(t)], inv_l[:, full(t)])
            )
            pl.when(goes_up(s))(lambda: x_copy(s, t).start())
            pl.when(goes_home(s))(lambda: home_copy(s, t).start())
            return carry

        lax.fori_loop(0, tiles, one, 0)

    def against_vec(high, low, block):
        return dot3t((high[...], low[...]), split(block))

    w_keep[0] = cov_rows[...]
    band_step(0)
    for c in inv_copies:
        c.wait_send()
    for c in cov_copies:
        c.start()
    for c in inv_copies:
        c.wait_recv()
    fill(inv_rows, inv_land, inv_h, inv_l)
    gain_step(0)

    sites = lax.broadcasted_iota(jnp.int32, (seen.shape[0], columns), 1)
    matches = jnp.where(sites == seen[...], 1.0, 0.0).astype(BF16)
    first, second = split(innovation[...])
    third = (innovation[...] - first.astype(F32) - second.astype(F32)).astype(BF16)
    pulled = jnp.zeros((VEC, columns), F32)
    for piece in (third, second, first):
        pulled = pulled + jnp.dot(piece, matches, preferred_element_type=F32)
    pulled = split(pulled)
    own = prior[...] + dot3t(pulled, split(cov_rows[...]))
    for c in prior_copies:
        c.wait()
    for c in cov_copies:
        c.wait()
    fill(cov_rows, cov_land, cov_h, cov_l)
    prior_row = jnp.concatenate([prior_all[r] for r in range(n_row)], axis=1)
    for t in range(tiles):
        cols = slice(t * TILE, (t + 1) * TILE)
        value = prior_row[:, cols] + dot3(pulled, (cov_h[:, cols], cov_l[:, cols]))
        h, l = split(value)
        f_h[:, EDGE + t * TILE : EDGE + (t + 1) * TILE] = h
        f_l[:, EDGE + t * TILE : EDGE + (t + 1) * TILE] = l
    zeros = jnp.zeros((VEC, EDGE), BF16)
    for ref in (f_h, f_l):
        ref[:, :EDGE] = zeros
        ref[:, EDGE + columns :] = zeros
    for t in range(tiles):
        wide = slice(t * TILE, t * TILE + window)
        h, l = split(dot3((f_h[:, wide], f_l[:, wide]), (ft_h[t], ft_l[t])))
        h_h[:, t * TILE : (t + 1) * TILE] = h
        h_l[:, t * TILE : (t + 1) * TILE] = l
    part[0] = own - against_vec(h_h, h_l, x_keep[0])

    @pl.when(tm == n - 1)
    def _():
        gain_out[...] = x_keep[0]

    inside = slice(EDGE, EDGE + columns)

    def forward(s, carry):
        @pl.when(tm >= s)
        def _():
            w_keep[s] = jnp.zeros((rows, columns), F32)

            def one(t, carry):
                x_copy(s - 1, t).wait_recv()
                piece = split(x_in[s - 1, :, full(t)])
                for c in range(0, columns, 2 * TILE):
                    cols = slice(c, c + 2 * TILE)
                    w_keep[s, :, cols] += dot3(
                        piece, (cov_h[full(t), cols], cov_l[full(t), cols])
                    )
                return carry

            lax.fori_loop(0, tiles, one, 0)
            band_step(s)
            gain_step(s)
            part[s] = dot3t(
                (f_h[:, inside], f_l[:, inside]), split(x_in[s - 1])
            ) - against_vec(h_h, h_l, x_keep[s])

        return carry

    lax.fori_loop(1, SPAN + 1, forward, 0)

    def backward(i, carry):
        s = SPAN - i

        @pl.when(tm >= s)
        def _():
            acc[...] = -x_keep[s]
            vec_out[s] = part[s]

            @pl.when((s < SPAN) & (tm < n - 1))
            def _():
                def one(t, carry):
                    v_copy(s + 1, t).wait_recv()
                    piece = split(v_in[s + 1, :, full(t)])
                    for c in range(0, columns, 2 * TILE):
                        cols = slice(c, c + 2 * TILE)
                        acc[:, cols] += dot3(
                            piece, (inv_h[full(t), cols], inv_l[full(t), cols])
                        )
                    return carry

                lax.fori_loop(0, tiles, one, 0)
                vec_copy(s + 1).wait_recv()
                vec_out[s] += vec_in[s + 1]

            pl.when(goes_down(s))(lambda: vec_copy(s).start())
            pad_acc[...] = jnp.zeros(pad_acc.shape, F32)
            for t in range(tiles):
                wide = slice(t * TILE, t * TILE + window)
                piece = split(acc[:, t * TILE : (t + 1) * TILE])
                pad_acc[:, wide] += dot3t(piece, (ft_h[t], ft_l[t]))
            h, l = split(pad_acc[:, inside])
            a_h[...] = h
            a_l[...] = l

            def last(t, carry):
                v_out[s, :, full(t)] = w_keep[s, :, full(t)] + dot3(
                    (a_h[...], a_l[...]), (cov_h[:, full(t)], cov_l[:, full(t)])
                )
                pl.when(goes_down(s))(lambda: v_copy(s, t).start())
                return carry

            lax.fori_loop(0, tiles, last, 0)

        return carry

    lax.fori_loop(0, SPAN + 1, backward, 0)
    spread_out[...] = v_out[0]
    shift_out[...] = vec_out[0]

    @pl.when(tm < n - 1)
    def _():
        for t in range(tiles):
            home_copy(1, t).wait_recv()

    for s in range(SPAN + 1):
        if s > 0:
            pl.when(goes_down(s))(lambda s=s: vec_copy(s).wait_send())
        for t in range(tiles):
            if s < SPAN:
                pl.when(goes_up(s))(lambda s=s, t=t: x_copy(s, t).wait_send())
            if s > 0:
                pl.when(goes_home(s))(lambda s=s, t=t: home_copy(s, t).wait_send())
                pl.when(goes_down(s))(lambda s=s, t=t: v_copy(s, t).wait_send())


def body(n, n_row, covariance, precision, band_weight, band_offset, prior_mean, innovation, seen_sites):
    rows, columns = covariance.shape[1:]
    tiles = columns // TILE
    window = TILE + 2 * EDGE
    steps = SPAN + 1
    block = lambda *lead: pltpu.VMEM(lead + (rows, columns), F32)
    whole = lambda kind: pltpu.VMEM((columns, columns), kind)
    vec = lambda *lead: pltpu.VMEM(lead + (VEC, rows), F32)
    padded = columns + 2 * EDGE
    copies = max(7, n_row - 1)
    dma = lambda *shape: pltpu.SemaphoreType.DMA(shape)
    vmem = pl.BlockSpec(memory_space=pltpu.VMEM)
    gain, shift, spread = pl.pallas_call(
        functools.partial(kernel, n, n_row),
        out_shape=(
            jax.ShapeDtypeStruct((rows, columns), F32),
            jax.ShapeDtypeStruct((VEC, rows), F32),
            jax.ShapeDtypeStruct((rows, columns), F32),
        ),
        in_specs=[pl.BlockSpec(memory_space=pltpu.SMEM)] + [vmem] * 6,
        out_specs=(vmem, vmem, vmem),
        scratch_shapes=[
            whole(F32), whole(F32),
            whole(BF16), whole(BF16), whole(BF16), whole(BF16),
            pltpu.VMEM((tiles, window, TILE), BF16), pltpu.VMEM((tiles, window, TILE), BF16),
            block(SPAN), block(steps), block(steps), block(steps), block(steps),
            pltpu.VMEM((rows, columns), BF16), pltpu.VMEM((rows, columns), BF16),
            pltpu.VMEM((rows, padded), BF16), pltpu.VMEM((rows, padded), BF16),
            block(), pltpu.VMEM((rows, padded), F32),
            vec(n_row),
            pltpu.VMEM((VEC, padded), BF16), pltpu.VMEM((VEC, padded), BF16),
            pltpu.VMEM((VEC, columns), BF16), pltpu.VMEM((VEC, columns), BF16),
            vec(steps), vec(steps), vec(steps),
            dma(2, copies), dma(2, copies), dma(n_row - 1), dma(n_row - 1),
            dma(SPAN, tiles), dma(SPAN, tiles), dma(steps, tiles), dma(tiles),
            dma(steps, tiles), dma(steps, tiles), dma(steps), dma(steps),
        ],
        compiler_params=pltpu.CompilerParams(
            collective_id=0, has_side_effects=True, vmem_limit_bytes=58 * 2**20
        ),
        cost_estimate=pl.CostEstimate(
            flops=2 * 54 * rows * columns * columns, bytes_accessed=16 * rows * columns,
            transcendentals=0,
        ),
    )(
        band_offset,
        covariance[0],
        precision[0],
        band_weight[0],
        jnp.broadcast_to(prior_mean, (VEC, rows)),
        jnp.broadcast_to(innovation, (VEC, innovation.shape[1])),
        seen_sites[0][:, None],
    )
    return gain[None], shift[:1], spread[None]


def solution(mesh):
    in_specs = (
        P("tm", "row", None),
        P("tm", "row", None),
        P("tm", None, None),
        P("tm", None),
        P("tm", "row"),
        P("tm", None),
        P("tm", None),
    )
    out_specs = (P("tm", "row", None), P("tm", "row"), P("tm", "row", None))
    return jax.shard_map(
        functools.partial(body, mesh.shape["tm"], mesh.shape["row"]),
        mesh=mesh, in_specs=in_specs, out_specs=out_specs, check_vma=False,
    )
```

profile of v0, /device:TPU:9, one launch (start us, length us, event | category | flops | bytes accessed | tf_op | source)
XLA Modules:
  0.0 161.3 jit_solution(3737910805062473759)
XLA Ops:
  0.6 0.0 copy-start.1
  0.6 1.3 broadcast_in_dim.23.innovation
  1.9 1.3 broadcast_in_dim.21.prior
  3.2 0.0 copy-done.1
  3.2 0.6 copy.13
  3.8 0.0 copy-start.2
  3.8 0.7 copy-done.2
  4.5 0.7 copy.10.seen
  5.2 151.4 %shard_map.94 = (f32[256,1024]{1,0:T(8,128)}, f32[16,256]{1,0:T(8,128)}, f32[256,1024]{1,0:T(8,128)}) custom-call(s32[1,5]{1,0:T(1,128)} %offsets.1, f32[256,1024]{1,0:T(8,128)} %bitcast.16, f32[256,1024]{1,0:T(8,128)} %bitcast.17, f32[5,1024]{1,0:T(8,128)} %bitcast.12, f32[16,256]{1,0:T(8,128)} %broadcast_in_dim.21.prior, ...), custom_call_target="tpu_custom_call" | custom-call | flops 28991029248 | bytes 4194304 | tf_op jit(solution)/shard_map/pallas_call | solution.py:391
  156.6 1.3 slice.3
  157.9 0.0 copy-start
  157.9 2.4 %copy.16 = f32[1,256,1024]{2,1,0:T(8,128)} copy(f32[1,256,1024]{2,1,0:T(8,128)} %bitcast.11) | data formatting | bytes 2097152
  160.3 0.0 copy-done
  160.3 1.0 copy.17
Async XLA Ops:
  0.6 2.5 %copy-start.1 = (f32[1,5,1024]{2,0,1:T(1,128)S(1)}, f32[1,5,1024]{2,0,1:T(1,128)}, u32[]{:S(2)}) copy-start(f32[1,5,1024]{2,0,1:T(1,128)} %param.9) | copy-start | bytes 61444
  3.8 0.7 copy-start.2
  157.9 2.4 %copy-start = (f32[256,1024]{1,0:T(8,128)S(1)}, f32[256,1024]{1,0:T(8,128)}, u32[]{:S(2)}) copy-start(f32[256,1024]{1,0:T(8,128)} %get-tuple-element.8) | copy-start | bytes 3145732
where the time goes:
time: 162 us; the launch traced here: 161 us
  Pallas kernels  151 us (93%)
  local copies, waits for them, and re-layouts  9.18 us (6%)
    pallas_call x1, Pallas kernels, body(): pl.pallas_call(functools.partial(kernel, n, n_row), out_shape=(jax.ShapeD...  151 us
    unnamed x9, local copies, waits for them, and re-layouts  4.65 us

commit v1 on v0

v1 whole, which is shorter than its diff:
```python
import functools

import jax
import jax.numpy as jnp
from jax import lax
from jax.experimental import pallas as pl
from jax.experimental.pallas import tpu as pltpu
from jax.sharding import PartitionSpec as P

NBAND = 5
REACH = 64
SPAN = 3
TILE = 256
EDGE = 128
VEC = 16

MESH = pl.DeviceIdType.MESH
F32 = jnp.float32
BF16 = jnp.bfloat16


def split(value):
    high = value.astype(BF16)
    return high, (value - high.astype(F32)).astype(BF16)


def dot3(left, right):
    (lh, ll), (rh, rl) = left, right
    one = functools.partial(jnp.dot, preferred_element_type=F32)
    return one(lh, rh) + (one(lh, rl) + one(ll, rh))


def dot3t(left, right):
    (lh, ll), (rh, rl) = left, right

    def one(a, b):
        return lax.dot_general(a, b, (((1,), (1,)), ((), ())), preferred_element_type=F32)

    return one(lh, rh) + (one(lh, rl) + one(ll, rh))


def kernel(
    n, n_row,
    offsets, cov_rows, inv_rows, weights, prior, innovation, seen,
    gain_out, shift_out, spread_out,
    land, rows_two, bands, cov_h, cov_l, inv_h, inv_l, ft_h, ft_l,
    x_in, x_keep, w_keep, v_in, v_out, a_h, a_l, pad_h, pad_l, acc, pad_acc,
    prior_all, means, f_h, f_l, h_h, h_l, part, vec_in, vec_out,
    g_send, g_recv, r_send, r_recv, s_send, s_recv, p_send, p_recv,
    x_send, x_recv, home_send, home_recv, v_send, v_recv, vec_send, vec_recv,
):
    tm = lax.axis_index("tm")
    row = lax.axis_index("row")
    rows, columns = cov_rows.shape
    tiles = columns // TILE
    even = lax.rem(tm, 2) == 0
    odd = lax.rem(tm, 2) == 1

    def at(index, size):
        return pl.ds(pl.multiple_of(index * size, size), size)

    def remote(src, dst, send, recv, to_tm, to_row):
        return pltpu.make_async_remote_copy(
            src_ref=src, dst_ref=dst, send_sem=send, recv_sem=recv,
            device_id=(to_tm, to_row), device_id_type=MESH,
        )

    barrier = pltpu.get_barrier_semaphore()

    def greet(t, r):
        pl.semaphore_signal(barrier, inc=1, device_id=(t, r), device_id_type=MESH)

    for d in range(1, n_row):
        greet(tm, lax.rem(row + d, n_row))
    for d in range(1, SPAN + 1):
        pl.when(tm + d < n)(lambda d=d: greet(tm + d, row))
        pl.when(tm - d >= 0)(lambda d=d: greet(tm - d, row))
    pl.semaphore_wait(
        barrier, n_row - 1 + jnp.minimum(tm, SPAN) + jnp.minimum(n - 1 - tm, SPAN)
    )

    twin = even & (tm >= 2) & (tm + 2 < n)
    lends = even & (tm >= 4)

    def valid(s):
        last = (odd & (tm >= SPAN)) | twin
        return ((s < SPAN) & (tm >= s)) | ((s == SPAN) & last)

    def goes_on(s):
        return valid(s) & (s < SPAN) & (tm + 1 < n)

    def goes_home(s):
        return valid(s) & (s > 0) & ((s == SPAN) | (tm == n - 1))

    def goes_back(s):
        return valid(s) & (s > 0)

    def chosen(s):
        return jnp.where((s == SPAN) & even, 1, 0)

    square = n_row == 4 and rows == TILE
    half = rows // 2
    if square:
        x, y = lax.rem(row, 2), row // 2
        r1, r2, r3 = 2 * y + 1 - x, 2 * (1 - y) + x, 2 * (1 - y) + 1 - x
        every, low, top = pl.ds(0, rows), pl.ds(0, half), pl.ds(half, half)
        right = pl.ds(pl.multiple_of(row * rows + half, half), half)
        right3 = pl.ds(pl.multiple_of(r3 * rows + half, half), half)
        plan = []
        for slot, to in enumerate((r1, r2, r3)):
            plan.append((to, slot, low, at(row, rows), every))
            plan.append((to, slot, top, right, top))
        plan.append((r1, 3, every, at(r2, rows), every))
        plan.append((r2, 4, every, at(r1, rows), every))
        plan.append((r1, 5, low, at(r3, rows), every))
        plan.append((r2, 6, every, right3, low))
    else:
        every = pl.ds(0, rows)
        wide = pl.ds(0, columns)
        plan = [
            (lax.rem(row + d, n_row), d - 1, every, wide, wide) for d in range(1, n_row)
        ]

    def gather(m, src):
        return [
            remote(
                src.at[rsl, csl], land.at[0, m, slot, rsl, dsl],
                g_send.at[m, c], g_recv.at[m, c], tm, to,
            )
            for c, (to, slot, rsl, csl, dsl) in enumerate(plan)
        ]

    def lend(m):
        return [
            remote(
                land.at[0, m, slot, rsl, dsl], land.at[1, m, slot, rsl, dsl],
                r_send.at[m, c], r_recv.at[m, c], tm - 2, row,
            )
            for c, (to, slot, rsl, csl, dsl) in enumerate(plan)
        ]

    def small(c, src, dst):
        return remote(src, dst, s_send.at[c], s_recv.at[c], tm - 2, row)

    lend_rows = [
        small(0, inv_rows, rows_two.at[0]), small(1, cov_rows, rows_two.at[1])
    ]
    lend_bands = small(2, bands.at[0], bands.at[1])
    lend_means = small(3, means.at[0], means.at[1])

    def fill(which, m, src, high, low_part):
        def put(rsl, csl, value):
            h, l = split(value)
            high[which, rsl, csl] = h
            low_part[which, rsl, csl] = l

        put(at(row, rows), pl.ds(0, columns), src[...])
        if not square:
            for d in range(1, n_row):
                owner = lax.rem(row + n_row - d, n_row)
                put(at(owner, rows), pl.ds(0, columns), land[which, m, d - 1])
            return
        for slot, r in enumerate((r1, r2, r3)):
            put(at(r, rows), at(row, rows), src[:, at(r, rows)].T)
            upper = pl.ds(pl.multiple_of(r * rows, half), half)
            lower = pl.ds(pl.multiple_of(r * rows + half, half), half)
            put(upper, at(r, rows), land[which, m, slot, :half, :])
            put(lower, lower, land[which, m, slot, half:, half:])
            put(lower, upper, land[which, m, slot, :half, half:].T)
        for slot, r in ((3, r1), (4, r2)):
            block = land[which, m, slot]
            put(at(r, rows), at(r3, rows), block)
            put(at(r3, rows), at(r, rows), block.T)
        upper = pl.ds(pl.multiple_of(r1 * rows, half), half)
        lower = pl.ds(pl.multiple_of(r1 * rows + half, half), half)
        block = land[which, m, 5, :half, :]
        put(upper, at(r2, rows), block)
        put(at(r2, rows), upper, block.T)
        block = land[which, m, 6, :, :half]
        put(at(r2, rows), lower, block)
        put(lower, at(r2, rows), block.T)

    inv_copies = gather(0, inv_rows)
    cov_copies = gather(1, cov_rows)
    for c in inv_copies:
        c.start()

    bands[0] = jnp.zeros(bands.shape[1:], F32)
    bands[0, :NBAND, :] = weights[...]
    for b in range(NBAND):
        bands[0, 8 + b : 9 + b, :] = jnp.full((1, columns), offsets[0, b].astype(F32))

    @pl.when(lends)
    def _():
        lend_bands.start()
        for c in lend_rows:
            c.start()

    vec_out[0] = jnp.broadcast_to(prior[...], (VEC, rows))
    prior_all[row] = vec_out[0]
    prior_copies = [
        remote(
            vec_out.at[0], prior_all.at[row], p_send.at[d - 1], p_recv.at[d - 1],
            tm, lax.rem(row + d, n_row),
        )
        for d in range(1, n_row)
    ]
    for c in prior_copies:
        c.start()

    window = TILE + 2 * EDGE

    def windows(which):
        apart = lax.broadcasted_iota(jnp.int32, (window, TILE), 0) - (
            lax.broadcasted_iota(jnp.int32, (window, TILE), 1) + EDGE
        )
        apart = apart.astype(F32)
        for t in range(tiles):
            cols = slice(t * TILE, (t + 1) * TILE)
            total = jnp.zeros((window, TILE), F32)
            for b in range(NBAND):
                hit = apart == bands[which, 8 + b : 9 + b, cols]
                total = total + jnp.where(hit, bands[which, b : b + 1, cols], 0.0)
            h, l = split(total)
            ft_h[which, t] = h
            ft_l[which, t] = l

    windows(0)

    zeros = jnp.zeros((rows, EDGE), BF16)
    for ref in (pad_h, pad_l):
        ref[:, :EDGE] = zeros
        ref[:, EDGE + columns :] = zeros

    def full(t):
        return pl.ds(pl.multiple_of(t * TILE, TILE), TILE)

    def x_copy(s, t):
        to = jnp.where((s == SPAN - 1) & odd, tm - 1, tm + 1)
        return remote(
            x_keep.at[s, :, full(t)], x_in.at[s, :, full(t)],
            x_send.at[s, t], x_recv.at[s, t], to, row,
        )

    def home_copy(s, t):
        to = tm - jnp.where((s == SPAN) & even, 1, s)
        return remote(
            x_keep.at[s, :, full(t)], gain_out.at[:, full(t)],
            home_send.at[s, t], home_recv.at[t], to, row,
        )

    def back_to(s):
        return jnp.where((s == SPAN) & even, tm + 1, tm - 1)

    def v_copy(s, t):
        return remote(
            v_out.at[s - 1, :, full(t)], v_in.at[s - 1, :, full(t)],
            v_send.at[s, t], v_recv.at[s, t], back_to(s), row,
        )

    def vec_copy(s):
        return remote(
            vec_out.at[s], vec_in.at[s], vec_send.at[s], vec_recv.at[s], back_to(s), row
        )

    def band_step(s, which):
        h, l = split(w_keep[s])
        pad_h[:, EDGE : EDGE + columns] = h
        pad_l[:, EDGE : EDGE + columns] = l
        for t in range(tiles):
            wide = slice(t * TILE, t * TILE + window)
            h, l = split(
                dot3((pad_h[:, wide], pad_l[:, wide]), (ft_h[which, t], ft_l[which, t]))
            )
            a_h[:, t * TILE : (t + 1) * TILE] = h
            a_l[:, t * TILE : (t + 1) * TILE] = l

    def gain_step(s, which):
        def one(t, carry):
            x_keep[s, :, full(t)] = dot3(
                (a_h[...], a_l[...]), (inv_h[which, :, full(t)], inv_l[which, :, full(t)])
            )
            pl.when(goes_on(s))(lambda: x_copy(s, t).start())
            early = goes_home(s) & ((s < SPAN) | (t < tiles // 2))
            pl.when(early)(lambda: home_copy(s, t).start())
            return carry

        lax.fori_loop(0, tiles, one, 0)

    w_keep[0] = cov_rows[...]
    band_step(0, 0)
    for c in inv_copies:
        c.wait_send()
    for c in cov_copies:
        c.start()
    for c in inv_copies:
        c.wait_recv()

    @pl.when(lends)
    def _():
        for c in lend(0):
            c.start()

    fill(0, 0, inv_rows, inv_h, inv_l)
    gain_step(0, 0)

    @pl.when(tm == n - 1)
    def _():
        gain_out[...] = x_keep[0]

    count = seen.shape[1]
    spots = jnp.broadcast_to(seen[...].astype(F32), (count, count)).T
    lanes = lax.broadcasted_iota(jnp.int32, (count, count), 1).astype(F32)
    matches = jnp.concatenate(
        [
            jnp.where(lanes + float(c * count) == spots, 1.0, 0.0)
            for c in range(columns // count)
        ],
        axis=1,
    ).astype(BF16)
    values = jnp.broadcast_to(innovation[...], (VEC, count))
    first, second = split(values)
    third = (values - first.astype(F32) - second.astype(F32)).astype(BF16)
    total = jnp.zeros((VEC, columns), F32)
    for piece in (third, second, first):
        total = total + jnp.dot(piece, matches, preferred_element_type=F32)
    pulled = split(total)
    own = vec_out[0] + dot3t(pulled, split(cov_rows[...]))
    for c in prior_copies:
        c.wait()
    for c in cov_copies:
        c.wait()

    @pl.when(lends)
    def _():
        for c in lend(1):
            c.start()

    fill(0, 1, cov_rows, cov_h, cov_l)
    inside = slice(EDGE, EDGE + columns)

    def cut_means(which):
        zeros = jnp.zeros((VEC, EDGE), BF16)
        h, l = split(means[which, 0])
        for ref, value in ((f_h, h), (f_l, l)):
            ref[which, :, :EDGE] = zeros
            ref[which, :, EDGE + columns :] = zeros
            ref[which, :, inside] = value

    def cut_moved(which):
        h, l = split(means[which, 1])
        h_h[which] = h
        h_l[which] = l

    def filtered():
        prior_row = jnp.concatenate([prior_all[r] for r in range(n_row)], axis=1)
        for t in range(tiles):
            cols = slice(t * TILE, (t + 1) * TILE)
            means[0, 0, :, cols] = prior_row[:, cols] + dot3(
                pulled, (cov_h[0, :, cols], cov_l[0, :, cols])
            )
        cut_means(0)
        for t in range(tiles):
            wide = slice(t * TILE, t * TILE + window)
            means[0, 1, :, t * TILE : (t + 1) * TILE] = dot3(
                (f_h[0, :, wide], f_l[0, :, wide]), (ft_h[0, t], ft_l[0, t])
            )
        cut_moved(0)
        pl.when(lends)(lambda: lend_means.start())

    def moved_part(s, which):
        return dot3t((h_h[which], h_l[which]), split(x_keep[s]))

    def forward(s, carry):
        which = chosen(s)

        @pl.when(twin & (s == SPAN))
        def _():
            for c in lend(1):
                c.wait_recv()
            lend_rows[1].wait_recv()
            fill(1, 1, rows_two.at[1], cov_h, cov_l)
            lend_means.wait_recv()
            cut_means(1)
            cut_moved(1)

        @pl.when(valid(s))
        def _():
            w_keep[s] = jnp.zeros((rows, columns), F32)

            def one(t, carry):
                x_copy(s - 1, t).wait_recv()
                piece = split(x_in[s - 1, :, full(t)])
                for c in range(0, columns, 2 * TILE):
                    cols = slice(c, c + 2 * TILE)
                    w_keep[s, :, cols] += dot3(
                        piece, (cov_h[which, full(t), cols], cov_l[which, full(t), cols])
                    )
                return carry

            lax.fori_loop(0, tiles, one, 0)
            band_step(s, which)
            gain_step(s, which)

        @pl.when(s == 1)
        def _():
            filtered()
            part[0] = own - moved_part(0, 0)

        @pl.when(valid(s))
        def _():
            part[s] = dot3t(
                (f_h[which, :, inside], f_l[which, :, inside]), split(x_in[s - 1])
            ) - moved_part(s, which)

        @pl.when(twin & (s == 1))
        def _():
            for c in lend(0):
                c.wait_recv()
            lend_rows[0].wait_recv()
            lend_bands.wait_recv()
            windows(1)
            fill(1, 0, rows_two.at[0], inv_h, inv_l)

        return carry

    lax.fori_loop(1, SPAN + 1, forward, 0)

    def backward(i, carry):
        s = SPAN - i
        which = chosen(s)

        @pl.when(valid(s))
        def _():
            acc[...] = -x_keep[s]
            vec_out[s] = part[s]

            @pl.when((s < SPAN) & (tm < n - 1))
            def _():
                def one(t, carry):
                    v_copy(s + 1, t).wait_recv()
                    piece = split(v_in[s, :, full(t)])
                    for c in range(0, columns, 2 * TILE):
                        cols = slice(c, c + 2 * TILE)
                        acc[:, cols] += dot3(
                            piece, (inv_h[0, full(t), cols], inv_l[0, full(t), cols])
                        )
                    return carry

                lax.fori_loop(0, tiles, one, 0)
                vec_copy(s + 1).wait_recv()
                vec_out[s] += vec_in[s + 1]

            pl.when(goes_back(s))(lambda: vec_copy(s).start())
            pad_acc[...] = jnp.zeros(pad_acc.shape, F32)
            for t in range(tiles):
                wide = slice(t * TILE, t * TILE + window)
                piece = split(acc[:, t * TILE : (t + 1) * TILE])
                pad_acc[:, wide] += dot3t(piece, (ft_h[which, t], ft_l[which, t]))
            h, l = split(pad_acc[:, inside])
            a_h[...] = h
            a_l[...] = l

            def last(t, carry):
                value = w_keep[s, :, full(t)] + dot3(
                    (a_h[...], a_l[...]), (cov_h[which, :, full(t)], cov_l[which, :, full(t)])
                )

                @pl.when(s > 0)
                def _():
                    v_out[s - 1, :, full(t)] = value
                    v_copy(s, t).start()

                @pl.when(s == 0)
                def _():
                    spread_out[:, full(t)] = value

                return carry

            lax.fori_loop(0, tiles, last, 0)

        @pl.when((s == 1) & valid(SPAN))
        def _():
            for t in range(tiles // 2, tiles):
                home_copy(SPAN, t).start()

        return carry

    lax.fori_loop(0, SPAN + 1, backward, 0)
    shift_out[...] = vec_out[0, :1, :]

    @pl.when(tm < n - 1)
    def _():
        for t in range(tiles):
            home_copy(1, t).wait_recv()

    @pl.when(lends)
    def _():
        for c in lend_rows + [lend_bands, lend_means] + lend(0) + lend(1):
            c.wait_send()

    for s in range(SPAN + 1):
        if s > 0:
            pl.when(goes_back(s))(lambda s=s: vec_copy(s).wait_send())
        for t in range(tiles):
            if s < SPAN:
                pl.when(goes_on(s))(lambda s=s, t=t: x_copy(s, t).wait_send())
            if s > 0:
                pl.when(goes_home(s))(lambda s=s, t=t: home_copy(s, t).wait_send())
                pl.when(goes_back(s))(lambda s=s, t=t: v_copy(s, t).wait_send())


def body(n, n_row, covariance, precision, band_weight, band_offset, prior_mean, innovation, seen_sites):
    rows, columns = covariance.shape[1:]
    tiles = columns // TILE
    window = TILE + 2 * EDGE
    steps = SPAN + 1
    square = n_row == 4 and rows == TILE
    copies = 10 if square else n_row - 1
    slots = (7, rows, rows) if square else (n_row - 1, rows, columns)
    block = lambda *lead: pltpu.VMEM(lead + (rows, columns), F32)
    whole = pltpu.VMEM((2, columns, columns), BF16)
    vec = lambda *lead: pltpu.VMEM(lead + (VEC, rows), F32)
    padded = columns + 2 * EDGE
    dma = lambda *shape: pltpu.SemaphoreType.DMA(shape)
    vmem = pl.BlockSpec(memory_space=pltpu.VMEM)
    gain, shift, spread = pl.pallas_call(
        functools.partial(kernel, n, n_row),
        out_shape=(
            jax.ShapeDtypeStruct((rows, columns), F32),
            jax.ShapeDtypeStruct((1, rows), F32),
            jax.ShapeDtypeStruct((rows, columns), F32),
        ),
        in_specs=[pl.BlockSpec(memory_space=pltpu.SMEM)] + [vmem] * 6,
        out_specs=(vmem, vmem, vmem),
        scratch_shapes=[
            pltpu.VMEM((2, 2) + slots, F32), block(2), pltpu.VMEM((2, 16, columns), F32),
            whole, whole, whole, whole,
            pltpu.VMEM((2, tiles, window, TILE), BF16), pltpu.VMEM((2, tiles, window, TILE), BF16),
            block(SPAN), block(steps), block(steps), block(SPAN), block(SPAN),
            pltpu.VMEM((rows, columns), BF16), pltpu.VMEM((rows, columns), BF16),
            pltpu.VMEM((rows, padded), BF16), pltpu.VMEM((rows, padded), BF16),
            block(), pltpu.VMEM((rows, padded), F32),
            vec(n_row), pltpu.VMEM((2, 2, VEC, columns), F32),
            pltpu.VMEM((2, VEC, padded), BF16), pltpu.VMEM((2, VEC, padded), BF16),
            pltpu.VMEM((2, VEC, columns), BF16), pltpu.VMEM((2, VEC, columns), BF16),
            vec(steps), vec(steps), vec(steps),
            dma(2, copies), dma(2, copies), dma(2, copies), dma(2, copies), dma(4), dma(4),
            dma(n_row - 1), dma(n_row - 1),
            dma(SPAN, tiles), dma(SPAN, tiles), dma(steps, tiles), dma(tiles),
            dma(steps, tiles), dma(steps, tiles), dma(steps), dma(steps),
        ],
        compiler_params=pltpu.CompilerParams(
            collective_id=0, has_side_effects=True, vmem_limit_bytes=62 * 2**20
        ),
        cost_estimate=pl.CostEstimate(
            flops=2 * 54 * rows * columns * columns, bytes_accessed=16 * rows * columns,
            transcendentals=0,
        ),
    )(
        band_offset, covariance[0], precision[0], band_weight[0],
        prior_mean, innovation, seen_sites,
    )
    return gain[None], shift, spread[None]


def solution(mesh):
    in_specs = (
        P("tm", "row", None),
        P("tm", "row", None),
        P("tm", None, None),
        P("tm", None),
        P("tm", "row"),
        P("tm", None),
        P("tm", None),
    )
    out_specs = (P("tm", "row", None), P("tm", "row"), P("tm", "row", None))
    return jax.shard_map(
        functools.partial(body, mesh.shape["tm"], mesh.shape["row"]),
        mesh=mesh, in_specs=in_specs, out_specs=out_specs, check_vma=False,
    )
```

time: 162 us -> 129 us (0.80)
  Pallas kernels: 151 us -> 123 us
  local copies, waits for them, and re-layouts: 9.18 us -> 5.29 us
    pallas_call x1, Pallas kernels: 151 us -> 123 us  [body(): pl.pallas_call(functools.partial(kernel, n, n_row), out_shape=(jax.ShapeD...]
    broadcast_in_dim x2 -> x0, local copies, waits for them, and re-layouts: 2.53 us -> none  [the longest x1 1.28 us: body(): jnp.broadcast_to(prior_mean, (VEC, rows))]
    unnamed x9 -> x8, local copies, waits for them, and re-layouts: 4.65 us -> 5.29 us
where the time goes in v1:
time: 129 us
  Pallas kernels  123 us (95%)
  local copies, waits for them, and re-layouts  5.29 us (4%)
    pallas_call x1, Pallas kernels, body(): pl.pallas_call(functools.partial(kernel, n, n_row), out_shape=(jax.ShapeD...  123 us
    unnamed x8, local copies, waits for them, and re-layouts  5.29 us

profile of v1, /device:TPU:9, one launch (start us, length us, event | category | flops | bytes accessed | tf_op | source)
XLA Modules:
  0.0 128.7 jit_solution(9180669278043462882)
XLA Ops:
  0.6 1.4 %copy.12 = f32[1,5,1024]{2,1,0:T(8,128)} copy(f32[1,5,1024]{2,0,1:T(1,128)} %param.9) | data formatting | bytes 40960
  2.0 122.7 %shard_map.94 = (f32[256,1024]{1,0:T(8,128)}, f32[1,256]{1,0:T(1,128)}, f32[256,1024]{1,0:T(8,128)}) custom-call(s32[1,5]{1,0:T(1,128)} %offsets.1, f32[256,1024]{1,0:T(8,128)} %bitcast.10, f32[256,1024]{1,0:T(8,128)} %bitcast.11, f32[5,1024]{1,0:T(8,128)} %bitcast.9, f32[1,256]{1,0:T(1,128)} %prior.1, f32[1,128]{1,0:T(1,128)} %innovation.1, s32[1,128]{1,0:T(1,128)} %seen.1), custom_call_target="tpu_custom_call" | custom-call | flops 28991029248 | bytes 4194304 | tf_op jit(solution)/shard_map/pallas_call | solution.py:527
  124.7 0.0 copy-start.1
  124.7 0.0 copy-start
  124.7 2.4 %copy.16 = f32[1,256,1024]{2,1,0:T(8,128)} copy(f32[1,256,1024]{2,1,0:T(8,128)} %bitcast.8) | data formatting | bytes 2097152
  127.1 0.0 copy-done.1
  127.1 0.6 copy.17
  127.7 0.0 copy-done
  127.7 1.0 copy.18
Async XLA Ops:
  124.7 2.4 %copy-start.1 = (f32[1,256]{1,0:T(1,128)S(1)}, f32[1,256]{1,0:T(1,128)}, u32[]{:S(2)}) copy-start(f32[1,256]{1,0:T(1,128)} %get-tuple-element.13) | copy-start | bytes 3076
  124.7 3.0 %copy-start = (f32[256,1024]{1,0:T(8,128)S(1)}, f32[256,1024]{1,0:T(8,128)}, u32[]{:S(2)}) copy-start(f32[256,1024]{1,0:T(8,128)} %get-tuple-element.8) | copy-start | bytes 3145732

commit v2 on v1

--- a/solution.py
+++ b/solution.py
@@ -24,19 +24,27 @@
     return high, (value - high.astype(F32)).astype(BF16)
 
 
+def stack(value):
+    return jnp.concatenate(split(value), axis=0)
+
+
 def dot3(left, right):
-    (lh, ll), (rh, rl) = left, right
+    high, low = right
     one = functools.partial(jnp.dot, preferred_element_type=F32)
-    return one(lh, rh) + (one(lh, rl) + one(ll, rh))
+    count = left.shape[0] // 2
+    both = one(left, high)
+    return both[:count] + (both[count:] + one(left[:count], low))
 
 
 def dot3t(left, right):
-    (lh, ll), (rh, rl) = left, right
+    high, low = right
 
     def one(a, b):
         return lax.dot_general(a, b, (((1,), (1,)), ((), ())), preferred_element_type=F32)
 
-    return one(lh, rh) + (one(lh, rl) + one(ll, rh))
+    count = left.shape[0] // 2
+    both = one(left, high)
+    return both[:count] + (both[count:] + one(left[:count], low))
 
 
 def kernel(
@@ -44,8 +52,8 @@
     offsets, cov_rows, inv_rows, weights, prior, innovation, seen,
     gain_out, shift_out, spread_out,
     land, rows_two, bands, cov_h, cov_l, inv_h, inv_l, ft_h, ft_l,
-    x_in, x_keep, w_keep, v_in, v_out, a_h, a_l, pad_h, pad_l, acc, pad_acc,
-    prior_all, means, f_h, f_l, h_h, h_l, part, vec_in, vec_out,
+    x_in, x_keep, w_keep, v_in, v_out, a_hl, pad_hl, acc, pad_acc,
+    prior_all, means, f_hl, h_hl, part, vec_in, vec_out,
     g_send, g_recv, r_send, r_recv, s_send, s_recv, p_send, p_recv,
     x_send, x_recv, home_send, home_recv, v_send, v_recv, vec_send, vec_recv,
 ):
@@ -148,37 +156,55 @@
     lend_bands = small(2, bands.at[0], bands.at[1])
     lend_means = small(3, means.at[0], means.at[1])
 
-    def fill(which, m, src, high, low_part):
+    def putter(which, high, low_part):
         def put(rsl, csl, value):
             h, l = split(value)
             high[which, rsl, csl] = h
             low_part[which, rsl, csl] = l
 
+        return put
+
+    def fill_own(which, src, high, low_part):
+        put = putter(which, high, low_part)
         put(at(row, rows), pl.ds(0, columns), src[...])
-        if not square:
-            for d in range(1, n_row):
-                owner = lax.rem(row + n_row - d, n_row)
-                put(at(owner, rows), pl.ds(0, columns), land[which, m, d - 1])
-            return
-        for slot, r in enumerate((r1, r2, r3)):
-            put(at(r, rows), at(row, rows), src[:, at(r, rows)].T)
-            upper = pl.ds(pl.multiple_of(r * rows, half), half)
-            lower = pl.ds(pl.multiple_of(r * rows + half, half), half)
-            put(upper, at(r, rows), land[which, m, slot, :half, :])
-            put(lower, lower, land[which, m, slot, half:, half:])
-            put(lower, upper, land[which, m, slot, :half, half:].T)
-        for slot, r in ((3, r1), (4, r2)):
-            block = land[which, m, slot]
-            put(at(r, rows), at(r3, rows), block)
-            put(at(r3, rows), at(r, rows), block.T)
-        upper = pl.ds(pl.multiple_of(r1 * rows, half), half)
-        lower = pl.ds(pl.multiple_of(r1 * rows + half, half), half)
-        block = land[which, m, 5, :half, :]
-        put(upper, at(r2, rows), block)
-        put(at(r2, rows), upper, block.T)
-        block = land[which, m, 6, :, :half]
-        put(at(r2, rows), lower, block)
-        put(lower, at(r2, rows), block.T)
+        if square:
+            for r in (r1, r2, r3):
+                put(at(r, rows), at(row, rows), src[:, at(r, rows)].T)
+
+    def fill_slots(which, m, copies, high, low_part, on=None):
+        put = putter(which, high, low_part)
+        for slot in range(7 if square else n_row - 1):
+            for c, entry in enumerate(plan):
+                if entry[1] == slot:
+                    copies[c].wait_recv()
+                    if on is not None:
+                        pl.when(lends)(lambda c=c: on[c].start())
+            if not square:
+                owner = lax.rem(row + n_row - 1 - slot, n_row)
+                put(at(owner, rows), pl.ds(0, columns), land[which, m, slot])
+            elif slot < 3:
+                r = (r1, r2, r3)[slot]
+                upper = pl.ds(pl.multiple_of(r * rows, half), half)
+                lower = pl.ds(pl.multiple_of(r * rows + half, half), half)
+                put(upper, at(r, rows), land[which, m, slot, :half, :])
+                put(lower, lower, land[which, m, slot, half:, half:])
+                put(lower, upper, land[which, m, slot, :half, half:].T)
+            elif slot < 5:
+                r = r1 if slot == 3 else r2
+                block = land[which, m, slot]
+                put(at(r, rows), at(r3, rows), block)
+                put(at(r3, rows), at(r, rows), block.T)
+            else:
+                upper = pl.ds(pl.multiple_of(r1 * rows, half), half)
+                lower = pl.ds(pl.multiple_of(r1 * rows + half, half), half)
+                if slot == 5:
+                    block = land[which, m, 5, :half, :]
+                    put(upper, at(r2, rows), block)
+                    put(at(r2, rows), upper, block.T)
+                else:
+                    block = land[which, m, 6, :, :half]
+                    put(at(r2, rows), lower, block)
+                    put(lower, at(r2, rows), block.T)
 
     inv_copies = gather(0, inv_rows)
     cov_copies = gather(1, cov_rows)
@@ -228,9 +254,9 @@
     windows(0)
 
     zeros = jnp.zeros((rows, EDGE), BF16)
-    for ref in (pad_h, pad_l):
-        ref[:, :EDGE] = zeros
-        ref[:, EDGE + columns :] = zeros
+    for first in (0, rows):
+        pad_hl[first : first + rows, :EDGE] = zeros
+        pad_hl[first : first + rows, EDGE + columns :] = zeros
 
     def full(t):
         return pl.ds(pl.multiple_of(t * TILE, TILE), TILE)
@@ -263,45 +289,45 @@
             vec_out.at[s], vec_in.at[s], vec_send.at[s], vec_recv.at[s], back_to(s), row
         )
 
+    pair = 2 * TILE
+
+    def two(c):
+        return pl.ds(pl.multiple_of(c * pair, pair), pair)
+
     def band_step(s, which):
         h, l = split(w_keep[s])
-        pad_h[:, EDGE : EDGE + columns] = h
-        pad_l[:, EDGE : EDGE + columns] = l
+        pad_hl[:rows, EDGE : EDGE + columns] = h
+        pad_hl[rows:, EDGE : EDGE + columns] = l
         for t in range(tiles):
             wide = slice(t * TILE, t * TILE + window)
-            h, l = split(
-                dot3((pad_h[:, wide], pad_l[:, wide]), (ft_h[which, t], ft_l[which, t]))
+            cols = slice(t * TILE, (t + 1) * TILE)
+            h, l = split(dot3(pad_hl[:, wide], (ft_h[which, t], ft_l[which, t])))
+            a_hl[:rows, cols] = h
+            a_hl[rows:, cols] = l
+
+    def gain_step(s, which):
+        def one(c, carry):
+            x_keep[s, :, two(c)] = dot3(
+                a_hl[...], (inv_h[which, :, two(c)], inv_l[which, :, two(c)])
             )
-            a_h[:, t * TILE : (t + 1) * TILE] = h
-            a_l[:, t * TILE : (t + 1) * TILE] = l
-
-    def gain_step(s, which):
-        def one(t, carry):
-            x_keep[s, :, full(t)] = dot3(
-                (a_h[...], a_l[...]), (inv_h[which, :, full(t)], inv_l[which, :, full(t)])
-            )
-            pl.when(goes_on(s))(lambda: x_copy(s, t).start())
-            early = goes_home(s) & ((s < SPAN) | (t < tiles // 2))
-            pl.when(early)(lambda: home_copy(s, t).start())
+            for i in range(2):
+                t = 2 * c + i
+                pl.when(goes_on(s))(lambda t=t: x_copy(s, t).start())
+                early = goes_home(s) & ((s < SPAN) | (t < tiles // 2))
+                pl.when(early)(lambda t=t: home_copy(s, t).start())
             return carry
 
-        lax.fori_loop(0, tiles, one, 0)
+        lax.fori_loop(0, tiles // 2, one, 0)
 
     w_keep[0] = cov_rows[...]
     band_step(0, 0)
+    fill_own(0, inv_rows, inv_h, inv_l)
+    fill_own(0, cov_rows, cov_h, cov_l)
     for c in inv_copies:
         c.wait_send()
     for c in cov_copies:
         c.start()
-    for c in inv_copies:
-        c.wait_recv()
-
-    @pl.when(lends)
-    def _():
-        for c in lend(0):
-            c.start()
-
-    fill(0, 0, inv_rows, inv_h, inv_l)
+    fill_slots(0, 0, inv_copies, inv_h, inv_l, lend(0))
     gain_step(0, 0)
 
     @pl.when(tm == n - 1)
@@ -324,33 +350,23 @@
     total = jnp.zeros((VEC, columns), F32)
     for piece in (third, second, first):
         total = total + jnp.dot(piece, matches, preferred_element_type=F32)
-    pulled = split(total)
+    pulled = stack(total)
     own = vec_out[0] + dot3t(pulled, split(cov_rows[...]))
     for c in prior_copies:
         c.wait()
+    fill_slots(0, 1, cov_copies, cov_h, cov_l, lend(1))
     for c in cov_copies:
-        c.wait()
-
-    @pl.when(lends)
-    def _():
-        for c in lend(1):
-            c.start()
-
-    fill(0, 1, cov_rows, cov_h, cov_l)
+        c.wait_send()
     inside = slice(EDGE, EDGE + columns)
 
     def cut_means(which):
-        zeros = jnp.zeros((VEC, EDGE), BF16)
-        h, l = split(means[which, 0])
-        for ref, value in ((f_h, h), (f_l, l)):
-            ref[which, :, :EDGE] = zeros
-            ref[which, :, EDGE + columns :] = zeros
-            ref[which, :, inside] = value
+        zeros = jnp.zeros((2 * VEC, EDGE), BF16)
+        f_hl[which, :, :EDGE] = zeros
+        f_hl[which, :, EDGE + columns :] = zeros
+        f_hl[which, :, inside] = stack(means[which, 0])
 
     def cut_moved(which):
-        h, l = split(means[which, 1])
-        h_h[which] = h
-        h_l[which] = l
+        h_hl[which] = stack(means[which, 1])
 
     def filtered():
         prior_row = jnp.concatenate([prior_all[r] for r in range(n_row)], axis=1)
@@ -363,23 +379,20 @@
         for t in range(tiles):
             wide = slice(t * TILE, t * TILE + window)
             means[0, 1, :, t * TILE : (t + 1) * TILE] = dot3(
-                (f_h[0, :, wide], f_l[0, :, wide]), (ft_h[0, t], ft_l[0, t])
+                f_hl[0, :, wide], (ft_h[0, t], ft_l[0, t])
             )
         cut_moved(0)
         pl.when(lends)(lambda: lend_means.start())
 
     def moved_part(s, which):
-        return dot3t((h_h[which], h_l[which]), split(x_keep[s]))
+        return dot3t(h_hl[which], split(x_keep[s]))
 
     def forward(s, carry):
         which = chosen(s)
 
         @pl.when(twin & (s == SPAN))
         def _():
-            for c in lend(1):
-                c.wait_recv()
-            lend_rows[1].wait_recv()
-            fill(1, 1, rows_two.at[1], cov_h, cov_l)
+            fill_slots(1, 1, lend(1), cov_h, cov_l)
             lend_means.wait_recv()
             cut_means(1)
             cut_moved(1)
@@ -390,7 +403,7 @@
 
             def one(t, carry):
                 x_copy(s - 1, t).wait_recv()
-                piece = split(x_in[s - 1, :, full(t)])
+                piece = stack(x_in[s - 1, :, full(t)])
                 for c in range(0, columns, 2 * TILE):
                     cols = slice(c, c + 2 * TILE)
                     w_keep[s, :, cols] += dot3(
@@ -409,18 +422,17 @@
 
         @pl.when(valid(s))
         def _():
-            part[s] = dot3t(
-                (f_h[which, :, inside], f_l[which, :, inside]), split(x_in[s - 1])
-            ) - moved_part(s, which)
+            part[s] = dot3t(f_hl[which, :, inside], split(x_in[s - 1])) - moved_part(s, which)
 
         @pl.when(twin & (s == 1))
         def _():
-            for c in lend(0):
-                c.wait_recv()
-            lend_rows[0].wait_recv()
             lend_bands.wait_recv()
             windows(1)
-            fill(1, 0, rows_two.at[0], inv_h, inv_l)
+            for c in lend_rows:
+                c.wait_recv()
+            fill_own(1, rows_two.at[0], inv_h, inv_l)
+            fill_own(1, rows_two.at[1], cov_h, cov_l)
+            fill_slots(1, 0, lend(0), inv_h, inv_l)
 
         return carry
 
@@ -439,7 +451,7 @@
             def _():
                 def one(t, carry):
                     v_copy(s + 1, t).wait_recv()
-                    piece = split(v_in[s, :, full(t)])
+                    piece = stack(v_in[s, :, full(t)])
                     for c in range(0, columns, 2 * TILE):
                         cols = slice(c, c + 2 * TILE)
                         acc[:, cols] += dot3(
@@ -455,29 +467,30 @@
             pad_acc[...] = jnp.zeros(pad_acc.shape, F32)
             for t in range(tiles):
                 wide = slice(t * TILE, t * TILE + window)
-                piece = split(acc[:, t * TILE : (t + 1) * TILE])
+                piece = stack(acc[:, t * TILE : (t + 1) * TILE])
                 pad_acc[:, wide] += dot3t(piece, (ft_h[which, t], ft_l[which, t]))
             h, l = split(pad_acc[:, inside])
-            a_h[...] = h
-            a_l[...] = l
-
-            def last(t, carry):
-                value = w_keep[s, :, full(t)] + dot3(
-                    (a_h[...], a_l[...]), (cov_h[which, :, full(t)], cov_l[which, :, full(t)])
+            a_hl[:rows] = h
+            a_hl[rows:] = l
+
+            def last(c, carry):
+                value = w_keep[s, :, two(c)] + dot3(
+                    a_hl[...], (cov_h[which, :, two(c)], cov_l[which, :, two(c)])
                 )
 
                 @pl.when(s > 0)
                 def _():
-                    v_out[s - 1, :, full(t)] = value
-                    v_copy(s, t).start()
+                    v_out[s - 1, :, two(c)] = value
+                    for i in range(2):
+                        v_copy(s, 2 * c + i).start()
 
                 @pl.when(s == 0)
                 def _():
-                    spread_out[:, full(t)] = value
+                    spread_out[:, two(c)] = value
 
                 return carry
 
-            lax.fori_loop(0, tiles, last, 0)
+            lax.fori_loop(0, tiles // 2, last, 0)
 
         @pl.when((s == 1) & valid(SPAN))
         def _():
@@ -538,12 +551,10 @@
             whole, whole, whole, whole,
             pltpu.VMEM((2, tiles, window, TILE), BF16), pltpu.VMEM((2, tiles, window, TILE), BF16),
             block(SPAN), block(steps), block(steps), block(SPAN), block(SPAN),
-            pltpu.VMEM((rows, columns), BF16), pltpu.VMEM((rows, columns), BF16),
-            pltpu.VMEM((rows, padded), BF16), pltpu.VMEM((rows, padded), BF16),
+            pltpu.VMEM((2 * rows, columns), BF16), pltpu.VMEM((2 * rows, padded), BF16),
             block(), pltpu.VMEM((rows, padded), F32),
             vec(n_row), pltpu.VMEM((2, 2, VEC, columns), F32),
-            pltpu.VMEM((2, VEC, padded), BF16), pltpu.VMEM((2, VEC, padded), BF16),
-            pltpu.VMEM((2, VEC, columns), BF16), pltpu.VMEM((2, VEC, columns), BF16),
+            pltpu.VMEM((2, 2 * VEC, padded), BF16), pltpu.VMEM((2, 2 * VEC, columns), BF16),
             vec(steps), vec(steps), vec(steps),
             dma(2, copies), dma(2, copies), dma(2, copies), dma(2, copies), dma(4), dma(4),
             dma(n_row - 1), dma(n_row - 1),

time: 129 us -> 130 us (level)
  no operation moved by 1% of the time
where the time goes in v2:
time: 130 us; the launch traced here: 129 us
  Pallas kernels  123 us (95%)
  local copies, waits for them, and re-layouts  5.29 us (4%)
    pallas_call x1, Pallas kernels, body(): pl.pallas_call(functools.partial(kernel, n, n_row), out_shape=(jax.ShapeD...  123 us
    unnamed x8, local copies, waits for them, and re-layouts  5.29 us

profile of v2, /device:TPU:9, one launch (start us, length us, event | category | flops | bytes accessed | tf_op | source)
XLA Modules:
  0.0 129.4 jit_solution(4252503871665130760)
XLA Ops:
  0.6 1.4 %copy.12 = f32[1,5,1024]{2,1,0:T(8,128)} copy(f32[1,5,1024]{2,0,1:T(1,128)} %param.9) | data formatting | bytes 40960
  2.0 123.5 %shard_map.94 = (f32[256,1024]{1,0:T(8,128)}, f32[1,256]{1,0:T(1,128)}, f32[256,1024]{1,0:T(8,128)}) custom-call(s32[1,5]{1,0:T(1,128)} %offsets.1, f32[256,1024]{1,0:T(8,128)} %bitcast.10, f32[256,1024]{1,0:T(8,128)} %bitcast.11, f32[5,1024]{1,0:T(8,128)} %bitcast.9, f32[1,256]{1,0:T(1,128)} %prior.1, f32[1,128]{1,0:T(1,128)} %innovation.1, s32[1,128]{1,0:T(1,128)} %seen.1), custom_call_target="tpu_custom_call" | custom-call | flops 28991029248 | bytes 4194304 | tf_op jit(solution)/shard_map/pallas_call | solution.py:540
  125.5 0.0 copy-start.1
  125.5 0.0 copy-start
  125.5 2.4 %copy.16 = f32[1,256,1024]{2,1,0:T(8,128)} copy(f32[1,256,1024]{2,1,0:T(8,128)} %bitcast.8) | data formatting | bytes 2097152
  127.9 0.0 copy-done.1
  127.9 0.6 copy.17
  128.5 0.0 copy-done
  128.5 1.0 copy.18
Async XLA Ops:
  125.5 2.4 %copy-start.1 = (f32[1,256]{1,0:T(1,128)S(1)}, f32[1,256]{1,0:T(1,128)}, u32[]{:S(2)}) copy-start(f32[1,256]{1,0:T(1,128)} %get-tuple-element.13) | copy-start | bytes 3076
  125.5 3.0 %copy-start = (f32[256,1024]{1,0:T(8,128)S(1)}, f32[256,1024]{1,0:T(8,128)}, u32[]{:S(2)}) copy-start(f32[256,1024]{1,0:T(8,128)} %get-tuple-element.8) | copy-start | bytes 3145732

commit v3 on v2

--- a/solution.py
+++ b/solution.py
@@ -147,11 +147,20 @@
             for c, (to, slot, rsl, csl, dsl) in enumerate(plan)
         ]
 
+    def share():
+        return [
+            remote(
+                rows_two.at[1, rsl, csl], land.at[1, 1, slot, rsl, dsl],
+                r_send.at[1, c], r_recv.at[1, c], tm, to,
+            )
+            for c, (to, slot, rsl, csl, dsl) in enumerate(plan)
+        ]
+
     def small(c, src, dst):
         return remote(src, dst, s_send.at[c], s_recv.at[c], tm - 2, row)
 
     lend_rows = [
-        small(0, inv_rows, rows_two.at[0]), small(1, cov_rows, rows_two.at[1])
+        small(1, cov_rows, rows_two.at[1]), small(0, inv_rows, rows_two.at[0])
     ]
     lend_bands = small(2, bands.at[0], bands.at[1])
     lend_means = small(3, means.at[0], means.at[1])
@@ -323,7 +332,8 @@
     band_step(0, 0)
     fill_own(0, inv_rows, inv_h, inv_l)
     fill_own(0, cov_rows, cov_h, cov_l)
-    for c in inv_copies:
+    ahead = len(plan) - 4 if square else len(plan)
+    for c in inv_copies[:ahead]:
         c.wait_send()
     for c in cov_copies:
         c.start()
@@ -354,9 +364,16 @@
     own = vec_out[0] + dot3t(pulled, split(cov_rows[...]))
     for c in prior_copies:
         c.wait()
-    fill_slots(0, 1, cov_copies, cov_h, cov_l, lend(1))
-    for c in cov_copies:
+    for c in inv_copies[ahead:] + cov_copies:
         c.wait_send()
+
+    @pl.when(twin)
+    def _():
+        lend_rows[0].wait_recv()
+        for c in share():
+            c.start()
+
+    fill_slots(0, 1, cov_copies, cov_h, cov_l)
     inside = slice(EDGE, EDGE + columns)
 
     def cut_means(which):
@@ -392,7 +409,6 @@
 
         @pl.when(twin & (s == SPAN))
         def _():
-            fill_slots(1, 1, lend(1), cov_h, cov_l)
             lend_means.wait_recv()
             cut_means(1)
             cut_moved(1)
@@ -428,11 +444,11 @@
         def _():
             lend_bands.wait_recv()
             windows(1)
-            for c in lend_rows:
-                c.wait_recv()
+            lend_rows[1].wait_recv()
             fill_own(1, rows_two.at[0], inv_h, inv_l)
+            fill_slots(1, 0, lend(0), inv_h, inv_l)
             fill_own(1, rows_two.at[1], cov_h, cov_l)
-            fill_slots(1, 0, lend(0), inv_h, inv_l)
+            fill_slots(1, 1, share(), cov_h, cov_l)
 
         return carry
 
@@ -509,7 +525,12 @@
 
     @pl.when(lends)
     def _():
-        for c in lend_rows + [lend_bands, lend_means] + lend(0) + lend(1):
+        for c in lend_rows + [lend_bands, lend_means] + lend(0):
+            c.wait_send()
+
+    @pl.when(twin)
+    def _():
+        for c in share():
             c.wait_send()
 
     for s in range(SPAN + 1):

time: 130 us -> 124 us (0.954)
  Pallas kernels: 123 us -> 117 us
    pallas_call x1, Pallas kernels: 123 us -> 117 us  [body(): pl.pallas_call(functools.partial(kernel, n, n_row), out_shape=(jax.ShapeD...]
where the time goes in v3:
time: 124 us; the launch traced here: 123 us
  Pallas kernels  117 us (94%)
  local copies, waits for them, and re-layouts  5.29 us (4%)
    pallas_call x1, Pallas kernels, body(): pl.pallas_call(functools.partial(kernel, n, n_row), out_shape=(jax.ShapeD...  117 us
    unnamed x8, local copies, waits for them, and re-layouts  5.29 us

profile of v3, /device:TPU:9, one launch (start us, length us, event | category | flops | bytes accessed | tf_op | source)
XLA Modules:
  0.0 123.0 jit_solution(6091054559034293295)
XLA Ops:
  0.6 1.4 %copy.12 = f32[1,5,1024]{2,1,0:T(8,128)} copy(f32[1,5,1024]{2,0,1:T(1,128)} %param.9) | data formatting | bytes 40960
  2.0 117.1 %shard_map.94 = (f32[256,1024]{1,0:T(8,128)}, f32[1,256]{1,0:T(1,128)}, f32[256,1024]{1,0:T(8,128)}) custom-call(s32[1,5]{1,0:T(1,128)} %offsets.1, f32[256,1024]{1,0:T(8,128)} %bitcast.10, f32[256,1024]{1,0:T(8,128)} %bitcast.11, f32[5,1024]{1,0:T(8,128)} %bitcast.9, f32[1,256]{1,0:T(1,128)} %prior.1, f32[1,128]{1,0:T(1,128)} %innovation.1, s32[1,128]{1,0:T(1,128)} %seen.1), custom_call_target="tpu_custom_call" | custom-call | flops 28991029248 | bytes 4194304 | tf_op jit(solution)/shard_map/pallas_call | solution.py:561
  119.1 0.0 copy-start.1
  119.1 0.0 copy-start
  119.1 2.4 %copy.16 = f32[1,256,1024]{2,1,0:T(8,128)} copy(f32[1,256,1024]{2,1,0:T(8,128)} %bitcast.8) | data formatting | bytes 2097152
  121.5 0.0 copy-done.1
  121.5 0.6 copy.17
  122.1 0.0 copy-done
  122.1 1.0 copy.18
Async XLA Ops:
  119.1 2.4 %copy-start.1 = (f32[1,256]{1,0:T(1,128)S(1)}, f32[1,256]{1,0:T(1,128)}, u32[]{:S(2)}) copy-start(f32[1,256]{1,0:T(1,128)} %get-tuple-element.13) | copy-start | bytes 3076
  119.1 3.0 %copy-start = (f32[256,1024]{1,0:T(8,128)S(1)}, f32[256,1024]{1,0:T(8,128)}, u32[]{:S(2)}) copy-start(f32[256,1024]{1,0:T(8,128)} %get-tuple-element.8) | copy-start | bytes 3145732

commit v4 on v3

--- a/solution.py
+++ b/solution.py
@@ -364,12 +364,20 @@
     own = vec_out[0] + dot3t(pulled, split(cov_rows[...]))
     for c in prior_copies:
         c.wait()
+    @pl.when(twin)
+    def _():
+        lend_bands.wait_recv()
+        windows(1)
+        for c in lend_rows:
+            c.wait_recv()
+        fill_own(1, rows_two.at[1], cov_h, cov_l)
+        fill_own(1, rows_two.at[0], inv_h, inv_l)
+
     for c in inv_copies[ahead:] + cov_copies:
         c.wait_send()
 
     @pl.when(twin)
     def _():
-        lend_rows[0].wait_recv()
         for c in share():
             c.start()
 
@@ -442,12 +450,7 @@
 
         @pl.when(twin & (s == 1))
         def _():
-            lend_bands.wait_recv()
-            windows(1)
-            lend_rows[1].wait_recv()
-            fill_own(1, rows_two.at[0], inv_h, inv_l)
             fill_slots(1, 0, lend(0), inv_h, inv_l)
-            fill_own(1, rows_two.at[1], cov_h, cov_l)
             fill_slots(1, 1, share(), cov_h, cov_l)
 
         return carry

time: 124 us -> 124 us (level)
  no operation moved by 1% of the time
where the time goes in v4:
time: 124 us; the launch traced here: 123 us
  Pallas kernels  117 us (94%)
  local copies, waits for them, and re-layouts  5.29 us (4%)
    pallas_call x1, Pallas kernels, body(): pl.pallas_call(functools.partial(kernel, n, n_row), out_shape=(jax.ShapeD...  117 us
    unnamed x8, local copies, waits for them, and re-layouts  5.29 us

profile of v4, /device:TPU:9, one launch (start us, length us, event | category | flops | bytes accessed | tf_op | source)
XLA Modules:
  0.0 123.0 jit_solution(6169216227832477554)
XLA Ops:
  0.6 1.4 %copy.12 = f32[1,5,1024]{2,1,0:T(8,128)} copy(f32[1,5,1024]{2,0,1:T(1,128)} %param.9) | data formatting | bytes 40960
  2.0 117.1 %shard_map.94 = (f32[256,1024]{1,0:T(8,128)}, f32[1,256]{1,0:T(1,128)}, f32[256,1024]{1,0:T(8,128)}) custom-call(s32[1,5]{1,0:T(1,128)} %offsets.1, f32[256,1024]{1,0:T(8,128)} %bitcast.10, f32[256,1024]{1,0:T(8,128)} %bitcast.11, f32[5,1024]{1,0:T(8,128)} %bitcast.9, f32[1,256]{1,0:T(1,128)} %prior.1, f32[1,128]{1,0:T(1,128)} %innovation.1, s32[1,128]{1,0:T(1,128)} %seen.1), custom_call_target="tpu_custom_call" | custom-call | flops 28991029248 | bytes 4194304 | tf_op jit(solution)/shard_map/pallas_call | solution.py:564
  119.1 0.0 copy-start.1
  119.1 0.0 copy-start
  119.1 2.4 %copy.16 = f32[1,256,1024]{2,1,0:T(8,128)} copy(f32[1,256,1024]{2,1,0:T(8,128)} %bitcast.8) | data formatting | bytes 2097152
  121.5 0.0 copy-done.1
  121.5 0.6 copy.17
  122.1 0.0 copy-done
  122.1 1.0 copy.18
Async XLA Ops:
  119.1 2.4 %copy-start.1 = (f32[1,256]{1,0:T(1,128)S(1)}, f32[1,256]{1,0:T(1,128)}, u32[]{:S(2)}) copy-start(f32[1,256]{1,0:T(1,128)} %get-tuple-element.13) | copy-start | bytes 3076
  119.1 3.0 %copy-start = (f32[256,1024]{1,0:T(8,128)S(1)}, f32[256,1024]{1,0:T(8,128)}, u32[]{:S(2)}) copy-start(f32[256,1024]{1,0:T(8,128)} %get-tuple-element.8) | copy-start | bytes 3145732

commit v5 on v4

--- a/solution.py
+++ b/solution.py
@@ -322,7 +322,7 @@
             for i in range(2):
                 t = 2 * c + i
                 pl.when(goes_on(s))(lambda t=t: x_copy(s, t).start())
-                early = goes_home(s) & ((s < SPAN) | (t < tiles // 2))
+                early = goes_home(s) & ((s < SPAN) | even | (t < tiles // 2))
                 pl.when(early)(lambda t=t: home_copy(s, t).start())
             return carry
 
@@ -412,7 +412,8 @@
     def moved_part(s, which):
         return dot3t(h_hl[which], split(x_keep[s]))
 
-    def forward(s, carry):
+    def forward(i, carry):
+        s = jnp.where(twin & (i > 1), SPAN + 2 - i, i)
         which = chosen(s)
 
         @pl.when(twin & (s == SPAN))
@@ -511,7 +512,7 @@
 
             lax.fori_loop(0, tiles // 2, last, 0)
 
-        @pl.when((s == 1) & valid(SPAN))
+        @pl.when((s == 1) & odd & valid(SPAN))
         def _():
             for t in range(tiles // 2, tiles):
                 home_copy(SPAN, t).start()

time: 124 us -> 125 us (level)
  the two profiles are of different devices: /device:TPU:9 before, /device:TPU:1 now
where the time goes in v5:
time: 125 us; the launch traced here: 124 us
  Pallas kernels  118 us (94%)
  local copies, waits for them, and re-layouts  5.29 us (4%)
    pallas_call x1, Pallas kernels, body(): pl.pallas_call(functools.partial(kernel, n, n_row), out_shape=(jax.ShapeD...  118 us
    unnamed x8, local copies, waits for them, and re-layouts  5.29 us

profile of v5, /device:TPU:1, one launch (start us, length us, event | category | flops | bytes accessed | tf_op | source)
XLA Modules:
  0.0 124.4 jit_solution(10679491155800318594)
XLA Ops:
  0.6 1.4 %copy.12 = f32[1,5,1024]{2,1,0:T(8,128)} copy(f32[1,5,1024]{2,0,1:T(1,128)} %param.9) | data formatting | bytes 40960
  2.0 118.5 %shard_map.94 = (f32[256,1024]{1,0:T(8,128)}, f32[1,256]{1,0:T(1,128)}, f32[256,1024]{1,0:T(8,128)}) custom-call(s32[1,5]{1,0:T(1,128)} %offsets.1, f32[256,1024]{1,0:T(8,128)} %bitcast.10, f32[256,1024]{1,0:T(8,128)} %bitcast.11, f32[5,1024]{1,0:T(8,128)} %bitcast.9, f32[1,256]{1,0:T(1,128)} %prior.1, f32[1,128]{1,0:T(1,128)} %innovation.1, s32[1,128]{1,0:T(1,128)} %seen.1), custom_call_target="tpu_custom_call" | custom-call | flops 28991029248 | bytes 4194304 | tf_op jit(solution)/shard_map/pallas_call | solution.py:565
  120.5 0.0 copy-start.1
  120.5 0.0 copy-start
  120.5 2.4 %copy.16 = f32[1,256,1024]{2,1,0:T(8,128)} copy(f32[1,256,1024]{2,1,0:T(8,128)} %bitcast.8) | data formatting | bytes 2097152
  122.9 0.0 copy-done.1
  122.9 0.6 copy.17
  123.4 0.0 copy-done
  123.4 1.0 copy.18
Async XLA Ops:
  120.5 2.4 %copy-start.1 = (f32[1,256]{1,0:T(1,128)S(1)}, f32[1,256]{1,0:T(1,128)}, u32[]{:S(2)}) copy-start(f32[1,256]{1,0:T(1,128)} %get-tuple-element.13) | copy-start | bytes 3076
  120.5 3.0 %copy-start = (f32[256,1024]{1,0:T(8,128)S(1)}, f32[256,1024]{1,0:T(8,128)}, u32[]{:S(2)}) copy-start(f32[256,1024]{1,0:T(8,128)} %get-tuple-element.8) | copy-start | bytes 3145732

commit v6 on v3

--- a/solution.py
+++ b/solution.py
@@ -32,8 +32,8 @@
     high, low = right
     one = functools.partial(jnp.dot, preferred_element_type=F32)
     count = left.shape[0] // 2
-    both = one(left, high)
-    return both[:count] + (both[count:] + one(left[:count], low))
+    top, rest = left[:count], left[count:]
+    return one(top, high) + (one(top, low) + one(rest, high))
 
 
 def dot3t(left, right):
@@ -43,8 +43,8 @@
         return lax.dot_general(a, b, (((1,), (1,)), ((), ())), preferred_element_type=F32)
 
     count = left.shape[0] // 2
-    both = one(left, high)
-    return both[:count] + (both[count:] + one(left[:count], low))
+    top, rest = left[:count], left[count:]
+    return one(top, high) + (one(top, low) + one(rest, high))
 
 
 def kernel(

time: 124 us -> 124 us (level)
  no operation moved by 1% of the time
where the time goes in v6:
time: 124 us; the launch traced here: 123 us
  Pallas kernels  117 us (94%)
  local copies, waits for them, and re-layouts  5.29 us (4%)
    pallas_call x1, Pallas kernels, body(): pl.pallas_call(functools.partial(kernel, n, n_row), out_shape=(jax.ShapeD...  117 us
    unnamed x8, local copies, waits for them, and re-layouts  5.29 us

profile of v6, /device:TPU:9, one launch (start us, length us, event | category | flops | bytes accessed | tf_op | source)
XLA Modules:
  0.0 123.2 jit_solution(13972516170318446879)
XLA Ops:
  0.6 1.4 %copy.12 = f32[1,5,1024]{2,1,0:T(8,128)} copy(f32[1,5,1024]{2,0,1:T(1,128)} %param.9) | data formatting | bytes 40960
  2.0 117.2 %shard_map.94 = (f32[256,1024]{1,0:T(8,128)}, f32[1,256]{1,0:T(1,128)}, f32[256,1024]{1,0:T(8,128)}) custom-call(s32[1,5]{1,0:T(1,128)} %offsets.1, f32[256,1024]{1,0:T(8,128)} %bitcast.10, f32[256,1024]{1,0:T(8,128)} %bitcast.11, f32[5,1024]{1,0:T(8,128)} %bitcast.9, f32[1,256]{1,0:T(1,128)} %prior.1, f32[1,128]{1,0:T(1,128)} %innovation.1, s32[1,128]{1,0:T(1,128)} %seen.1), custom_call_target="tpu_custom_call" | custom-call | flops 28991029248 | bytes 4194304 | tf_op jit(solution)/shard_map/pallas_call | solution.py:561
  119.2 0.0 copy-start.1
  119.2 0.0 copy-start
  119.2 2.4 %copy.16 = f32[1,256,1024]{2,1,0:T(8,128)} copy(f32[1,256,1024]{2,1,0:T(8,128)} %bitcast.8) | data formatting | bytes 2097152
  121.6 0.0 copy-done.1
  121.6 0.6 copy.17
  122.2 0.0 copy-done
  122.2 1.0 copy.18
Async XLA Ops:
  119.2 2.4 %copy-start.1 = (f32[1,256]{1,0:T(1,128)S(1)}, f32[1,256]{1,0:T(1,128)}, u32[]{:S(2)}) copy-start(f32[1,256]{1,0:T(1,128)} %get-tuple-element.13) | copy-start | bytes 3076
  119.2 3.0 %copy-start = (f32[256,1024]{1,0:T(8,128)S(1)}, f32[256,1024]{1,0:T(8,128)}, u32[]{:S(2)}) copy-start(f32[256,1024]{1,0:T(8,128)} %get-tuple-element.8) | copy-start | bytes 3145732
